TPU v7x, 128 devices: a whole 4x4x4 slice. The times are simulated.
128 devices in a mesh: row: 8 (over y_hi, x), col: 16 (over y_lo, z, core).
Axes of the slice: x: 4, y: 4 (y_hi: 2, y_lo: 2; y = y_hi * 2 + y_lo), z: 4, core: 2. Of those that a mesh axis runs over, the one named last changes fastest.
Arguments:
- alignment_embedding: bfloat16 [256, 640, 256], P(('row', 'col')), may hold values from -6 to 6
- standardizer_scaling: float32 [256], replicated, may hold values from 0.1 to 1.9
- first_linear_map: bfloat16 [256, 32], replicated, may hold values from -0.375 to 0.375
- first_offset_terms: float32 [32], replicated, may hold values from -0.6 to 0.6
- second_linear_map: bfloat16 [256, 32], replicated, may hold values from -0.375 to 0.375
- second_offset_terms: float32 [32], replicated, may hold values from -0.6 to 0.6
- final_linear_map: bfloat16 [1024, 128], replicated, may hold values from -4 to 4
- final_offset_terms: float32 [128], replicated, may hold values from -3 to 3
- couple_embedding: bfloat16 [640, 640, 128], P('row', 'col'), may hold values from -6 to 6
Outputs:
- pair_out: bfloat16 [640, 640, 128], P('row', 'col')
All inputs are finite; a program needn't handle non-finite values.
Results may differ from a plain program's by a relative error of at most 0.0067.
Values may be sent and summed in bfloat16 or wider, within the bound.
A program may use at most 128 MiB of HBM per device.

v0:
```python
import jax
import jax.numpy as jnp
from jax import lax
from jax.experimental import pallas as pl
from jax.experimental.pallas import tpu as pltpu
from jax.sharding import PartitionSpec as P

BF = jnp.bfloat16
F32 = jnp.float32
MESH = pl.DeviceIdType.MESH

SEQ = 2
RES = 640
FEAT = 256
HID = 32
CP = 128
NROW, NCOL = 8, 16
TOTAL = SEQ * NROW * NCOL
ROWS = RES // NROW
COLS = RES // NCOL
LB, LC = ROWS // 16, HID // 8
LT = LB * LC
RG = COLS // 4
LPAY, RPAY = 48, 32
CHUNK = 160


def spot(at, **step):
    size = dict(yh=2, x=4, yl=2, z=4, k=2)
    to = {a: lax.rem(at[a] + step[a], size[a]) if a in step else at[a] for a in at}
    return to["yh"] * 4 + to["x"], (to["yl"] * 4 + to["z"]) * 2 + to["k"]


def kernel(
    x_hbm, scale_ref, w1_ref, b1_ref, w2_ref, b2_ref, wf_hbm, bf_ref, pair_hbm, out_hbm,
    x_v, wf_v, pair_v, out_v, proj, pay_f, lpay, rpay, lrecv, rrecv, left, right,
    lt, rp, xk, bd, acc,
    load_sem, s1_send, s1_recv, l_send, l_recv, r_send, r_recv, k_send, k_recv,
):
    row, col = lax.axis_index("row"), lax.axis_index("col")
    at = dict(yh=row // 4, x=row % 4, yl=col // 8, z=(col // 2) % 4, k=col % 2)

    loads = [
        pltpu.make_async_copy(x_hbm, x_v, load_sem.at[0]),
        pltpu.make_async_copy(wf_hbm, wf_v, load_sem.at[1]),
        pltpu.make_async_copy(pair_hbm, pair_v, load_sem.at[2]),
    ]
    for load in loads:
        load.start()

    row_peers = [lax.rem(row + k, NROW) for k in range(1, NROW)]
    col_peers = [lax.rem(col + k, NCOL) for k in range(1, NCOL)]
    barrier = pltpu.get_barrier_semaphore()
    for r in row_peers:
        pl.semaphore_signal(barrier, inc=1, device_id=(r, col), device_id_type=MESH)
    for c in col_peers:
        pl.semaphore_signal(barrier, inc=1, device_id=(row, c), device_id_type=MESH)

    wide = lax.broadcasted_iota(jnp.int32, (512, HID), 0) // 16
    sel_l = (wide == lax.broadcasted_iota(jnp.int32, (512, HID), 1)).astype(F32)
    wide = lax.broadcasted_iota(jnp.int32, (128, HID), 0) % 32
    sel_r = (wide == lax.broadcasted_iota(jnp.int32, (128, HID), 1)).astype(F32)
    w_l = jnp.dot(sel_l.astype(BF), w1_ref[...], preferred_element_type=F32).astype(BF)
    w_r = jnp.dot(sel_r.astype(BF), w2_ref[...], preferred_element_type=F32).astype(BF)
    across = (((1,), (1,)), ((), ()))
    exact = dict(precision=lax.Precision.HIGHEST, preferred_element_type=F32)
    b_l = lax.dot_general(b1_ref[...], sel_l, across, **exact)
    b_r = lax.dot_general(b2_ref[...], sel_r, across, **exact)
    scale = scale_ref[...]

    loads[0].wait()

    def norm(i, carry):
        rows = pl.ds(pl.multiple_of(i * CHUNK, CHUNK), CHUNK)
        x = x_v[rows, :].astype(F32)
        mean = jnp.sum(x, axis=1, keepdims=True) * (1.0 / FEAT)
        dev = x - mean
        var = jnp.sum(dev * dev, axis=1, keepdims=True) * (1.0 / FEAT)
        normed = (dev * lax.rsqrt(var + 1e-5) * scale).astype(BF)
        p_l = lax.dot_general(normed, w_l, across, preferred_element_type=F32)
        for c4 in range(LC):
            proj[c4, rows, :] = p_l[:, c4 * 128 : c4 * 128 + 128]
        proj[LC, rows, :] = lax.dot_general(
            normed, w_r, across, preferred_element_type=F32
        )
        return carry

    lax.fori_loop(0, SEQ * RES // CHUNK, norm, 0)

    lane = lax.broadcasted_iota(jnp.int32, (LB, 128), 1) % 16
    for r in range(NROW):
        for s in range(SEQ):
            for c4 in range(LC):
                lanes = slice(c4 * 128, c4 * 128 + 128)
                got = proj[c4, pl.ds(s * RES + r * ROWS, LB, stride=16), :]
                for p in range(1, 16):
                    piece = proj[c4, pl.ds(s * RES + r * ROWS + p, LB, stride=16), :]
                    got = jnp.where(lane == p, piece, got)
                pay_f[pl.ds(r * LPAY + (s * LC + c4) * LB, LB), :] = got + b_l[:, lanes]
    lpay[...] = pay_f[: NROW * LPAY, :].astype(BF).reshape(NROW, LPAY, 128)

    pl.semaphore_wait(barrier, len(row_peers) + len(col_peers))
    s1_l = []
    for k, r in enumerate(row_peers):
        s1_l.append(
            pltpu.make_async_remote_copy(
                src_ref=lpay.at[r], dst_ref=lrecv.at[row],
                send_sem=s1_send.at[k], recv_sem=s1_recv.at[k],
                device_id=(r, col), device_id_type=MESH,
            )
        )
        s1_l[-1].start()
    lrecv[row] = lpay[row]

    lane = lax.broadcasted_iota(jnp.int32, (RG, 128), 1) // 32
    for c in range(NCOL):
        for s in range(SEQ):
            got = proj[LC, pl.ds(s * RES + c * COLS, RG, stride=4), :]
            for p in range(1, 4):
                piece = proj[LC, pl.ds(s * RES + c * COLS + p, RG, stride=4), :]
                got = jnp.where(lane == p, piece, got)
            pay_f[pl.ds(c * RPAY + s * RG, RG), :] = got + b_r
    rpay[...] = pay_f[: NCOL * RPAY, :].astype(BF).reshape(NCOL, RPAY, 128)
    s1_r = []
    for k, c in enumerate(col_peers):
        s1_r.append(
            pltpu.make_async_remote_copy(
                src_ref=rpay.at[c], dst_ref=rrecv.at[col],
                send_sem=s1_send.at[NROW - 1 + k], recv_sem=s1_recv.at[NROW - 1 + k],
                device_id=(row, c), device_id_type=MESH,
            )
        )
        s1_r[-1].start()
    rrecv[col] = rpay[col]

    loads[1].wait()
    bd[...] = jnp.zeros_like(bd)

    def spread(c, carry):
        rows = wf_v[pl.ds(pl.multiple_of(c * HID, HID), HID), :]
        for q in range(4):
            bd[pl.ds(pl.multiple_of(c * 128 + q * 32, 32), 32), q * 128 : q * 128 + 128] = rows
        return carry

    lax.fori_loop(0, HID, spread, 0)

    def sender(ref, sends, recvs):
        def send(n, slot, part, **step):
            block = ref.at[slot] if part is None else ref.at[slot, part]
            copy = pltpu.make_async_remote_copy(
                src_ref=block, dst_ref=block, send_sem=sends.at[n], recv_sem=recvs.at[n],
                device_id=spot(at, **step), device_id_type=MESH,
            )
            copy.start()
            return copy

        return send

    send_l = sender(left, l_send, l_recv)
    send_k = sender(left, k_send, k_recv)
    send_r = sender(right, r_send, r_recv)

    def lslot(yl, z):
        return (lax.rem(at["yl"] + yl, 2) * 4 + lax.rem(at["z"] + z, 4)) * 2 + at["k"]

    def rslot(yh, x):
        return lax.rem(at["yh"] + yh, 2) * 4 + lax.rem(at["x"] + x, 4)

    la, lb = pl.ds(0, LT // 2), pl.ds(LT // 2, LT // 2)
    ra, rb = pl.ds(0, RG // 2), pl.ds(RG // 2, RG // 2)
    lcp, rcp, kcp = {}, {}, {}

    for copy in s1_l:
        copy.wait_recv()
    pay_f[: NROW * LPAY, :] = lrecv[...].reshape(NROW * LPAY, 128).astype(F32)
    for b in range(LB):
        for c4 in range(LC):
            parts = [
                pay_f[pl.ds((s * LC + c4) * LB + b, NROW, stride=LPAY), :] for s in range(SEQ)
            ]
            left[col, b * LC + c4] = jnp.concatenate(parts, axis=0).astype(BF)
    lcp[0] = send_l(0, lslot(0, 0), None, yl=1)
    lcp[1] = send_l(1, lslot(0, 0), None, z=1)
    lcp[2] = send_l(2, lslot(0, 0), None, z=3)
    kcp[0] = send_k(0, lslot(0, 0), None, k=1)

    for copy in s1_r:
        copy.wait_recv()
    pay_f[: NCOL * RPAY, :] = rrecv[...].reshape(NCOL * RPAY, 128).astype(F32)
    for g in range(RG):
        parts = [pay_f[pl.ds(s * RG + g, NCOL, stride=RPAY), :] for s in range(SEQ)]
        right[row, g] = jnp.concatenate(parts, axis=0).astype(BF)
    rcp[0] = send_r(0, rslot(0, 0), None, yh=1)
    rcp[1] = send_r(1, rslot(0, 0), None, x=1)
    rcp[2] = send_r(2, rslot(0, 0), None, x=3)

    lcp[0].wait_recv()
    lcp[3] = send_l(3, lslot(1, 0), None, z=1)
    lcp[4] = send_l(4, lslot(1, 0), None, z=3)
    kcp[1] = send_k(1, lslot(1, 0), None, k=1)
    rcp[0].wait_recv()
    rcp[3] = send_r(3, rslot(1, 0), None, x=1)
    rcp[4] = send_r(4, rslot(1, 0), None, x=3)
    for y in range(2):
        near = 1 if y == 0 else 3
        lcp[near].wait_recv()
        lcp[5 + 2 * y] = send_l(5 + 2 * y, lslot(y, 3), la, z=1)
        kcp[2 + 2 * y] = send_k(2 + 2 * y, lslot(y, 3), None, k=1)
        rcp[near].wait_recv()
        rcp[5 + 2 * y] = send_r(5 + 2 * y, rslot(y, 3), ra, x=1)
        lcp[near + 1].wait_recv()
        lcp[6 + 2 * y] = send_l(6 + 2 * y, lslot(y, 1), lb, z=3)
        kcp[3 + 2 * y] = send_k(3 + 2 * y, lslot(y, 1), None, k=1)
        rcp[near + 1].wait_recv()
        rcp[6 + 2 * y] = send_r(6 + 2 * y, rslot(y, 1), rb, x=3)
    for y in range(2):
        lcp[5 + 2 * y].wait_recv()
        kcp[6 + 2 * y] = send_k(6 + 2 * y, lslot(y, 2), la, k=1)
        lcp[6 + 2 * y].wait_recv()
        kcp[7 + 2 * y] = send_k(7 + 2 * y, lslot(y, 2), lb, k=1)
    for y in range(2):
        rcp[5 + 2 * y].wait_recv()
        rcp[6 + 2 * y].wait_recv()

    new = lax.broadcasted_iota(jnp.int32, (TOTAL, TOTAL), 0)
    old = lax.broadcasted_iota(jnp.int32, (TOTAL, TOTAL), 1)
    perm = ((new % 8) * 32 + (new // 8) % 2 * 16 + new // 16 == old).astype(F32).astype(BF)
    for g in range(RG):
        block = right[:, g].reshape(TOTAL, 128)
        rp[:, g * 128 : g * 128 + 128] = jnp.dot(
            perm, block, preferred_element_type=F32
        ).astype(BF)

    for n in range(10):
        kcp[n].wait_recv()

    def turn(t, carry):
        lt[pl.ds(pl.multiple_of(t * 128, 128), 128), :] = jnp.transpose(
            left[:, t].reshape(TOTAL, 128)
        )
        return carry

    lax.fori_loop(0, LT, turn, 0, unroll=4)

    def outer(b, carry):
        for n in range(RG // 2):
            for h in range(2):
                x = jnp.dot(
                    lt[pl.ds(pl.multiple_of(b * 512, 512) + h * 256, 256), :],
                    rp[:, n * 256 : n * 256 + 256],
                    preferred_element_type=F32,
                ).astype(BF)
                for c in range(16):
                    for g in range(2):
                        at_row = pl.multiple_of((2 * n + g) * ROWS + b * 16, 16)
                        at_lane = (h * 16 + c) * 128
                        xk[pl.ds(at_row, 16), at_lane : at_lane + 128] = x[
                            c * 16 : c * 16 + 16, g * 128 : g * 128 + 128
                        ]
        return carry

    lax.fori_loop(0, LB, outer, 0)

    per = 5 * ROWS

    def project(m, carry):
        r = jnp.dot(
            xk[pl.ds(pl.multiple_of(m * per, per), per), :], bd[...], preferred_element_type=F32
        )
        for g in range(5):
            for q in range(4):
                acc[pl.ds(m * 20 + g * 4 + q, ROWS, stride=COLS), :] = r[
                    g * ROWS : g * ROWS + ROWS, q * 128 : q * 128 + 128
                ]
        return carry

    lax.fori_loop(0, 2, project, 0)

    loads[2].wait()
    bias = bf_ref[...]

    def finish(i, carry):
        rows = pl.ds(pl.multiple_of(i * 320, 320), 320)
        update = acc[rows, :] * (1.0 / TOTAL) + bias
        out_v[rows, :] = (pair_v[rows, :].astype(F32) + update).astype(BF)
        return carry

    lax.fori_loop(0, ROWS * COLS // 320, finish, 0)
    store = pltpu.make_async_copy(out_v, out_hbm, load_sem.at[0])
    store.start()
    for copy in s1_l + s1_r + list(lcp.values()) + list(rcp.values()) + list(kcp.values()):
        copy.wait_send()
    store.wait()


def body(x, scale, w1, b1, w2, b2, wf, bf, pair):
    vmem = pl.BlockSpec(memory_space=pltpu.VMEM)
    hbm = pl.BlockSpec(memory_space=pl.ANY)
    dma = pltpu.SemaphoreType.DMA
    n1 = NROW + NCOL - 2
    out = pl.pallas_call(
        kernel,
        out_shape=jax.ShapeDtypeStruct((ROWS * COLS, CP), BF),
        in_specs=[hbm, vmem, vmem, vmem, vmem, vmem, hbm, vmem, hbm],
        out_specs=hbm,
        scratch_shapes=[
            pltpu.VMEM((SEQ * RES, FEAT), BF),
            pltpu.VMEM((HID * HID, CP), BF),
            pltpu.VMEM((ROWS * COLS, CP), BF),
            pltpu.VMEM((ROWS * COLS, CP), BF),
            pltpu.VMEM((5, SEQ * RES, 128), F32),
            pltpu.VMEM((NCOL * RPAY, 128), F32),
            pltpu.VMEM((NROW, LPAY, 128), BF),
            pltpu.VMEM((NCOL, RPAY, 128), BF),
            pltpu.VMEM((NROW, LPAY, 128), BF),
            pltpu.VMEM((NCOL, RPAY, 128), BF),
            pltpu.VMEM((NCOL, LT, SEQ * NROW, 128), BF),
            pltpu.VMEM((NROW, RG, SEQ * NCOL, 128), BF),
            pltpu.VMEM((ROWS * HID, TOTAL), BF),
            pltpu.VMEM((TOTAL, COLS * HID), BF),
            pltpu.VMEM((RG * ROWS, HID * 128), BF),
            pltpu.VMEM((HID * 128, 4 * CP), BF),
            pltpu.VMEM((ROWS * COLS, CP), F32),
            dma((3,)), dma((n1,)), dma((n1,)),
            dma((9,)), dma((9,)), dma((9,)), dma((9,)), dma((10,)), dma((10,)),
        ],
        compiler_params=pltpu.CompilerParams(
            collective_id=0, has_side_effects=True, vmem_limit_bytes=56 * 2**20
        ),
    )(
        x.reshape(SEQ * RES, FEAT), scale.reshape(1, FEAT), w1.T, b1.reshape(1, HID),
        w2.T, b2.reshape(1, HID), wf, bf.reshape(1, CP), pair.reshape(ROWS * COLS, CP),
    )
    return out.reshape(ROWS, COLS, CP)


def solution(mesh):
    return jax.shard_map(
        body,
        mesh=mesh,
        in_specs=(P(("row", "col"), None, None), P(), P(), P(), P(), P(), P(), P(), P("row", "col", None)),
        out_specs=P("row", "col", None),
        check_vma=False,
    )
```

profile of v0, /device:TPU:1, one launch (start us, length us, event | category | flops | bytes accessed | tf_op | source)
XLA Modules:
  0.0 40.6 jit_solution(9789233254906010251)
XLA Ops:
  0.0 38.5 %shard_map.91 = bf16[3200,128]{1,0:T(8,128)(2,1)} custom-call(bf16[1280,256]{1,0:T(8,128)(2,1)} %bitcast.11, f32[1,256]{1,0:T(1,128)} %bitcast.14, bf16[32,256]{1,0:T(8,128)(2,1)} %bitcast.12, f32[1,32]{1,0:T(1,128)} %bitcast.15, bf16[32,256]{1,0:T(8,128)(2,1)} %bitcast.13, f32[1,32]{1,0:T(1,128)} %bitcast.16, bf16[1024,128]{1,0:T(8,128)(2,1)} %wf_hbm.1, ...), custom_call_target="tpu_custom_call" | custom-call | tf_op jit(solution)/shard_map/pallas_call | solution.py:301
  38.5 2.1 %copy.11 = bf16[80,40,128]{2,1,0:T(8,128)(2,1)} copy(bf16[80,40,128]{2,1,0:T(8,128)(2,1)} %bitcast.9) | data formatting | bytes 1638400
where the time goes:
time: 40.9 us; the launch traced here: 40.6 us
  Pallas kernels  38.5 us (94%)
  local copies, waits for them, and re-layouts  2.11 us (5%)
    pallas_call x1, Pallas kernels, body(): pl.pallas_call(kernel, out_shape=jax.ShapeDtypeStruct((ROWS * COLS, CP),...  38.5 us
    unnamed x1, local copies, waits for them, and re-layouts  2.11 us

commit v1 on v0

v1 whole, which is shorter than its diff:
```python
import jax
import jax.numpy as jnp
from jax import lax
from jax.experimental import pallas as pl
from jax.experimental.pallas import tpu as pltpu
from jax.sharding import PartitionSpec as P

BF = jnp.bfloat16
F32 = jnp.float32
MESH = pl.DeviceIdType.MESH

SEQ = 2
RES = 640
FEAT = 256
HID = 32
CP = 128
NROW, NCOL = 8, 16
TOTAL = SEQ * NROW * NCOL
ROWS = RES // NROW
COLS = RES // NCOL
LB, LC = ROWS // 16, HID // 8
LT = LB * LC
RG = COLS // 4
PARTS = ((0, 3), (3, 5))
LPAY, RPAY = 48, 32
CHUNK = 160


def spot(at, **step):
    size = dict(yh=2, x=4, yl=2, z=4, k=2)
    to = {a: lax.rem(at[a] + step[a], size[a]) if a in step else at[a] for a in at}
    return to["yh"] * 4 + to["x"], (to["yl"] * 4 + to["z"]) * 2 + to["k"]


def kernel(
    x_hbm, scale_hbm, w1_hbm, b1_hbm, w2_hbm, b2_hbm, wf_hbm, bf_hbm, out_ref,
    x_v, scale_ref, w1_ref, b1_ref, w2_ref, b2_ref, wf_v, bf_ref, proj, pay_f, lpay, rpay, lrecv, rrecv, left, right,
    lt, rp, xk, bd,
    load_sem, s1_send, s1_recv, l_send, l_recv, r_send, r_recv, k_send, k_recv,
):
    row, col = lax.axis_index("row"), lax.axis_index("col")
    at = dict(yh=row // 4, x=row % 4, yl=col // 8, z=(col // 2) % 4, k=col % 2)

    loads = [
        pltpu.make_async_copy(source, held, load_sem.at[n])
        for n, (source, held) in enumerate((
            (w1_hbm, w1_ref), (w2_hbm, w2_ref), (b1_hbm, b1_ref), (b2_hbm, b2_ref),
            (scale_hbm, scale_ref), (x_hbm, x_v), (wf_hbm, wf_v), (bf_hbm, bf_ref),
        ))
    ]
    for load in loads:
        load.start()

    row_peers = [lax.rem(row + k, NROW) for k in range(1, NROW)]
    col_peers = [lax.rem(col + k, NCOL) for k in range(1, NCOL)]
    barrier = pltpu.get_barrier_semaphore()
    for r in row_peers:
        pl.semaphore_signal(barrier, inc=1, device_id=(r, col), device_id_type=MESH)
    for c in col_peers:
        pl.semaphore_signal(barrier, inc=1, device_id=(row, c), device_id_type=MESH)

    for load in loads[:5]:
        load.wait()
    wide = lax.broadcasted_iota(jnp.int32, (512, HID), 0) // 16
    sel_l = (wide == lax.broadcasted_iota(jnp.int32, (512, HID), 1)).astype(F32)
    wide = lax.broadcasted_iota(jnp.int32, (128, HID), 0) % 32
    sel_r = (wide == lax.broadcasted_iota(jnp.int32, (128, HID), 1)).astype(F32)
    w_l = jnp.dot(sel_l.astype(BF), w1_ref[...], preferred_element_type=F32).astype(BF)
    w_r = jnp.dot(sel_r.astype(BF), w2_ref[...], preferred_element_type=F32).astype(BF)
    across = (((1,), (1,)), ((), ()))
    exact = dict(precision=lax.Precision.HIGHEST, preferred_element_type=F32)
    b_l = lax.dot_general(b1_ref[...], sel_l, across, **exact)
    b_r = lax.dot_general(b2_ref[...], sel_r, across, **exact)
    scale = scale_ref[...]

    loads[5].wait()

    def norm(i, carry):
        rows = pl.ds(pl.multiple_of(i * CHUNK, CHUNK), CHUNK)
        x = x_v[rows, :].astype(F32)
        mean = jnp.sum(x, axis=1, keepdims=True) * (1.0 / FEAT)
        dev = x - mean
        var = jnp.sum(dev * dev, axis=1, keepdims=True) * (1.0 / FEAT)
        normed = (dev * lax.rsqrt(var + 1e-5) * scale).astype(BF)
        p_l = lax.dot_general(normed, w_l, across, preferred_element_type=F32)
        for c4 in range(LC):
            proj[c4, rows, :] = p_l[:, c4 * 128 : c4 * 128 + 128]
        proj[LC, rows, :] = lax.dot_general(
            normed, w_r, across, preferred_element_type=F32
        )
        return carry

    lax.fori_loop(0, SEQ * RES // CHUNK, norm, 0, unroll=4)

    lane = lax.broadcasted_iota(jnp.int32, (LB, 128), 1) % 16
    for r in range(NROW):
        for s in range(SEQ):
            for c4 in range(LC):
                lanes = slice(c4 * 128, c4 * 128 + 128)
                got = proj[c4, pl.ds(s * RES + r * ROWS, LB, stride=16), :]
                for p in range(1, 16):
                    piece = proj[c4, pl.ds(s * RES + r * ROWS + p, LB, stride=16), :]
                    got = jnp.where(lane == p, piece, got)
                pay_f[pl.ds(r * LPAY + (s * LC + c4) * LB, LB), :] = got + b_l[:, lanes]
    lpay[...] = pay_f[: NROW * LPAY, :].astype(BF).reshape(NROW, LPAY, 128)

    pl.semaphore_wait(barrier, len(row_peers) + len(col_peers))
    s1_l = []
    for k, r in enumerate(row_peers):
        s1_l.append(
            pltpu.make_async_remote_copy(
                src_ref=lpay.at[r], dst_ref=lrecv.at[row],
                send_sem=s1_send.at[k], recv_sem=s1_recv.at[k],
                device_id=(r, col), device_id_type=MESH,
            )
        )
        s1_l[-1].start()
    lrecv[row] = lpay[row]

    lane = lax.broadcasted_iota(jnp.int32, (RG, 128), 1) // 32
    for c in range(NCOL):
        for s in range(SEQ):
            got = proj[LC, pl.ds(s * RES + c * COLS, RG, stride=4), :]
            for p in range(1, 4):
                piece = proj[LC, pl.ds(s * RES + c * COLS + p, RG, stride=4), :]
                got = jnp.where(lane == p, piece, got)
            pay_f[pl.ds(c * RPAY + s * RG, RG), :] = got + b_r
    rpay[...] = pay_f[: NCOL * RPAY, :].astype(BF).reshape(NCOL, RPAY, 128)
    s1_r = []
    for k, c in enumerate(col_peers):
        s1_r.append(
            pltpu.make_async_remote_copy(
                src_ref=rpay.at[c], dst_ref=rrecv.at[col],
                send_sem=s1_send.at[NROW - 1 + k], recv_sem=s1_recv.at[NROW - 1 + k],
                device_id=(row, c), device_id_type=MESH,
            )
        )
        s1_r[-1].start()
    rrecv[col] = rpay[col]

    loads[6].wait()
    loads[7].wait()
    bd[...] = jnp.zeros_like(bd)

    def spread(c, carry):
        rows = wf_v[pl.ds(pl.multiple_of(c * HID, HID), HID), :]
        for q in range(4):
            bd[pl.ds(pl.multiple_of(c * 128 + q * 32, 32), 32), q * 128 : q * 128 + 128] = rows
        return carry

    lax.fori_loop(0, HID, spread, 0)

    me_k, me_l = at["k"], at["yl"] * 4 + at["z"]
    sends_l, sends_r, sends_k = {}, {}, {}

    def send_l(part, y, way, **step):
        lo, hi = PARTS[part]
        slot = lax.rem(at["yl"] + y, 2) * 4 + at["z"]
        block = left.at[pl.ds(lo, hi - lo), me_k, slot]
        n = len(sends_l)
        copy = pltpu.make_async_remote_copy(
            src_ref=block, dst_ref=block, send_sem=l_send.at[n], recv_sem=l_recv.at[n],
            device_id=spot(at, **step), device_id_type=MESH,
        )
        copy.start()
        sends_l[part, y, way] = copy

    def send_r(y, way, **step):
        block = right.at[lax.rem(at["yh"] + y, 2) * 4 + at["x"]]
        n = len(sends_r)
        copy = pltpu.make_async_remote_copy(
            src_ref=block, dst_ref=block, send_sem=r_send.at[n], recv_sem=r_recv.at[n],
            device_id=spot(at, **step), device_id_type=MESH,
        )
        copy.start()
        sends_r[y, way] = copy

    def send_k(part):
        lo, hi = PARTS[part]
        block = left.at[pl.ds(lo, hi - lo), me_k]
        copy = pltpu.make_async_remote_copy(
            src_ref=block, dst_ref=block, send_sem=k_send.at[part], recv_sem=k_recv.at[part],
            device_id=spot(at, k=1), device_id_type=MESH,
        )
        copy.start()
        sends_k[part] = copy

    def ring_l(part, y):
        for step in (1, 3, 2):
            send_l(part, y, step, z=step)

    def ring_r(y):
        for step in (1, 3, 2):
            send_r(y, step, x=step)

    def arrived_l(part):
        for y in range(2):
            for step in (1, 3, 2):
                sends_l[part, y, step].wait_recv()
        send_k(part)

    for copy in s1_l:
        copy.wait_recv()
    pay_f[: NROW * LPAY, :] = lrecv[...].reshape(NROW * LPAY, 128).astype(F32)
    for b in range(LB):
        for c4 in range(LC):
            parts = [
                pay_f[pl.ds((s * LC + c4) * LB + b, NROW, stride=LPAY), :] for s in range(SEQ)
            ]
            left[b, me_k, me_l, c4] = jnp.concatenate(parts, axis=0).astype(BF)
    send_l(0, 0, "y", yl=1)
    ring_l(0, 0)

    for copy in s1_r:
        copy.wait_recv()
    pay_f[: NCOL * RPAY, :] = rrecv[...].reshape(NCOL * RPAY, 128).astype(F32)
    for g in range(RG):
        parts = [pay_f[pl.ds(s * RG + g, NCOL, stride=RPAY), :] for s in range(SEQ)]
        right[row, g] = jnp.concatenate(parts, axis=0).astype(BF)
    send_r(0, "y", yh=1)
    ring_r(0)

    sends_l[0, 0, "y"].wait_recv()
    ring_l(0, 1)
    send_l(1, 0, "y", yl=1)
    sends_r[0, "y"].wait_recv()
    ring_r(1)
    ring_l(1, 0)
    sends_l[1, 0, "y"].wait_recv()
    ring_l(1, 1)

    arrived_l(0)
    for y in range(2):
        for step in (1, 3, 2):
            sends_r[y, step].wait_recv()

    new = lax.broadcasted_iota(jnp.int32, (TOTAL, TOTAL), 0)
    old = lax.broadcasted_iota(jnp.int32, (TOTAL, TOTAL), 1)
    from_old = new % 8 * 32 + new // 8 % 2 * 16 + new // 16 % 8 * 2 + new // 128
    perm = (from_old == old).astype(F32).astype(BF)
    for g in range(RG):
        block = right[:, g].reshape(TOTAL, 128)
        rp[:, g * 128 : g * 128 + 128] = jnp.dot(
            perm, block, preferred_element_type=F32
        ).astype(BF)

    def outer(b, carry):
        for c4 in range(LC):
            lt[pl.ds(pl.multiple_of(b * 512, 512) + c4 * 128, 128), :] = jnp.transpose(
                left[b, :, :, c4].reshape(TOTAL, 128)
            )
        for n in range(RG // 2):
            for h in range(2):
                x = jnp.dot(
                    lt[pl.ds(pl.multiple_of(b * 512, 512) + h * 256, 256), :],
                    rp[:, n * 256 : n * 256 + 256],
                    preferred_element_type=F32,
                ).astype(BF)
                for c in range(16):
                    for g in range(2):
                        at_row = pl.multiple_of(b * 16 * RG, 16) + (2 * n + g) * 16
                        at_lane = (h * 16 + c) * 128
                        xk[pl.ds(at_row, 16), at_lane : at_lane + 128] = x[
                            c * 16 : c * 16 + 16, g * 128 : g * 128 + 128
                        ]
        return carry

    def project(part):
        lo, hi = PARTS[part]
        r = jnp.dot(
            xk[lo * 16 * RG : hi * 16 * RG, :], bd[...], preferred_element_type=F32
        ) * (1.0 / TOTAL)
        for b in range(hi - lo):
            for g in range(RG):
                for q in range(4):
                    at_row = (lo + b) * 16 * COLS + g * 4 + q
                    from_row = (b * RG + g) * 16
                    out_ref[pl.ds(at_row, 16, stride=COLS), :] = r[
                        from_row : from_row + 16, q * 128 : q * 128 + 128
                    ] + bf_ref[...]

    sends_k[0].wait_recv()
    lax.fori_loop(*PARTS[0], outer, 0)
    arrived_l(1)
    project(0)
    sends_k[1].wait_recv()
    lax.fori_loop(*PARTS[1], outer, 0)
    project(1)

    sent = s1_l + s1_r + list(sends_l.values()) + list(sends_r.values()) + list(sends_k.values())
    for copy in sent:
        copy.wait_send()


def body(x, scale, w1, b1, w2, b2, wf, bf, pair):
    vmem = pl.BlockSpec(memory_space=pltpu.VMEM)
    hbm = pl.BlockSpec(memory_space=pltpu.HBM)
    dma = pltpu.SemaphoreType.DMA
    n1 = NROW + NCOL - 2
    acc = pl.pallas_call(
        kernel,
        out_shape=pltpu.VMEM((ROWS * COLS, CP), F32),
        in_specs=[hbm] * 8,
        out_specs=vmem,
        scratch_shapes=[
            pltpu.VMEM((SEQ * RES, FEAT), BF),
            pltpu.VMEM((1, FEAT), F32),
            pltpu.VMEM((HID, FEAT), BF),
            pltpu.VMEM((1, HID), F32),
            pltpu.VMEM((HID, FEAT), BF),
            pltpu.VMEM((1, HID), F32),
            pltpu.VMEM((HID * HID, CP), BF),
            pltpu.VMEM((1, CP), F32),
            pltpu.VMEM((5, SEQ * RES, 128), F32),
            pltpu.VMEM((NCOL * RPAY, 128), F32),
            pltpu.VMEM((NROW, LPAY, 128), BF),
            pltpu.VMEM((NCOL, RPAY, 128), BF),
            pltpu.VMEM((NROW, LPAY, 128), BF),
            pltpu.VMEM((NCOL, RPAY, 128), BF),
            pltpu.VMEM((LB, 2, 8, LC, SEQ * NROW, 128), BF),
            pltpu.VMEM((NROW, RG, SEQ * NCOL, 128), BF),
            pltpu.VMEM((ROWS * HID, TOTAL), BF),
            pltpu.VMEM((TOTAL, COLS * HID), BF),
            pltpu.VMEM((RG * ROWS, HID * 128), BF),
            pltpu.VMEM((HID * 128, 4 * CP), BF),
            dma((8,)), dma((n1,)), dma((n1,)),
            dma((14,)), dma((14,)), dma((7,)), dma((7,)), dma((2,)), dma((2,)),
        ],
        compiler_params=pltpu.CompilerParams(
            collective_id=0, has_side_effects=True, vmem_limit_bytes=56 * 2**20
        ),
    )(
        x.reshape(SEQ * RES, FEAT), scale.reshape(1, FEAT), w1.T, b1.reshape(1, HID),
        w2.T, b2.reshape(1, HID), wf, bf.reshape(1, CP),
    )
    return (pair.astype(F32) + acc.reshape(ROWS, COLS, CP)).astype(BF)


def solution(mesh):
    return jax.shard_map(
        body,
        mesh=mesh,
        in_specs=(P(("row", "col"), None, None), P(), P(), P(), P(), P(), P(), P(), P("row", "col", None)),
        out_specs=P("row", "col", None),
        check_vma=False,
    )
```

time: 40.9 us -> 33.5 us (0.82)
  Pallas kernels: 38.5 us -> 32.3 us
  local copies, waits for them, and re-layouts: 2.11 us -> 0.01 us
  other arithmetic: 0 us -> 1.05 us
    pallas_call x1, Pallas kernels: 38.5 us -> 32.3 us  [body(): pl.pallas_call(kernel, out_shape=pltpu.VMEM((ROWS * COLS, CP), F32), in_s...]
    unnamed x1 -> x2, local copies, waits for them, and re-layouts: 2.11 us -> 0.01 us
    convert_element_type x0 -> x1, other arithmetic: none -> 1.05 us  [body(): return (pair.astype(F32) + acc.reshape(ROWS, COLS, CP)).astype(BF)]
where the time goes in v1:
time: 33.5 us; the launch traced here: 33.4 us
  Pallas kernels  32.3 us (96%)
  other arithmetic  1.05 us (3%)
    pallas_call x1, Pallas kernels, body(): pl.pallas_call(kernel, out_shape=pltpu.VMEM((ROWS * COLS, CP), F32), in_s...  32.3 us
    convert_element_type x1, other arithmetic, body(): return (pair.astype(F32) + acc.reshape(ROWS, COLS, CP)).astype(BF)  1.05 us

profile of v1, /device:TPU:1, one launch (start us, length us, event | category | flops | bytes accessed | tf_op | source)
XLA Modules:
  0.0 33.4 jit_solution(16852187478677505996)
XLA Ops:
  0.0 0.0 copy-start
  0.0 32.3 %shard_map.91 = f32[3200,128]{1,0:T(8,128)S(1)} custom-call(bf16[1280,256]{1,0:T(8,128)(2,1)} %bitcast.9, f32[1,256]{1,0:T(1,128)} %bitcast.12, bf16[32,256]{1,0:T(8,128)(2,1)} %bitcast.10, f32[1,32]{1,0:T(1,128)} %bitcast.13, bf16[32,256]{1,0:T(8,128)(2,1)} %bitcast.11, f32[1,32]{1,0:T(1,128)} %bitcast.14, bf16[1024,128]{1,0:T(8,128)(2,1)} %wf_hbm.1, ...), custom_call_target="tpu_custom_call" | custom-call | tf_op jit(solution)/shard_map/pallas_call | solution.py:300
  32.3 0.0 copy-done
  32.3 1.1 %add_convert_fusion = bf16[80,40,128]{2,1,0:T(8,128)(2,1)} fusion(f32[80,40,128]{2,1,0:T(8,128)S(1)} %bitcast.8, bf16[80,40,128]{2,1,0:T(8,128)(2,1)S(1)} %copy-done), kind=kLoop, calls=%fused_computation | loop fusion | flops 1228800 | bytes 3276800 | tf_op jit(solution)/shard_map/convert_element_type | solution.py:336
Async XLA Ops:
  0.0 32.3 %copy-start = (bf16[80,40,128]{2,1,0:T(8,128)(2,1)S(1)}, bf16[80,40,128]{2,1,0:T(8,128)(2,1)}, u32[]{:S(2)}) copy-start(bf16[80,40,128]{2,1,0:T(8,128)(2,1)} %param.17) | copy-start | bytes 2457604

commit v2 on v1

v2 whole, which is shorter than its diff:
```python
import jax
import jax.numpy as jnp
from jax import lax
from jax.experimental import pallas as pl
from jax.experimental.pallas import tpu as pltpu
from jax.sharding import PartitionSpec as P

BF = jnp.bfloat16
F32 = jnp.float32
MESH = pl.DeviceIdType.MESH

SEQ = 2
RES = 640
FEAT = 256
HID = 32
CP = 128
NROW, NCOL = 8, 16
TOTAL = SEQ * NROW * NCOL
ROWS = RES // NROW
COLS = RES // NCOL
LB, LC = ROWS // 16, HID // 8
LT = LB * LC
RG = COLS // 4
RING = (2, 1, 3)
PARTS = ((0, 3), (3, 5))
LPAY, RPAY = 48, 32
CHUNK = 320


def spot(at, **step):
    size = dict(yh=2, x=4, yl=2, z=4, k=2)
    to = {a: lax.rem(at[a] + step[a], size[a]) if a in step else at[a] for a in at}
    return to["yh"] * 4 + to["x"], (to["yl"] * 4 + to["z"]) * 2 + to["k"]


def kernel(
    x_hbm, scale_hbm, w1_hbm, b1_hbm, w2_hbm, b2_hbm, wf_hbm, bf_hbm, out_ref,
    x_v, scale_ref, w1_ref, b1_ref, w2_ref, b2_ref, wf_v, bf_ref, proj, pay_f, lpay, rpay, lrecv, rrecv, left, right,
    lt, rp, xk, bd,
    load_sem, s1_send, s1_recv, l_send, l_recv, r_send, r_recv, k_send, k_recv,
):
    row, col = lax.axis_index("row"), lax.axis_index("col")
    at = dict(yh=row // 4, x=row % 4, yl=col // 8, z=(col // 2) % 4, k=col % 2)

    loads = [
        pltpu.make_async_copy(source, held, load_sem.at[n])
        for n, (source, held) in enumerate((
            (w1_hbm, w1_ref), (w2_hbm, w2_ref), (b1_hbm, b1_ref), (b2_hbm, b2_ref),
            (scale_hbm, scale_ref), (x_hbm, x_v), (wf_hbm, wf_v), (bf_hbm, bf_ref),
        ))
    ]
    for load in loads:
        load.start()

    other = lax.rem(col + NCOL // 2, NCOL)
    l_peers = [(k, lax.rem(row + k, NROW), c) for c in (col, other) for k in range(NROW)][1:]
    r_peers = [lax.rem(col + k, NCOL) for k in range(1, NCOL)]
    greet = [(r, c) for k, r, c in l_peers if k > 0] + [(row, c) for c in r_peers]
    barrier = pltpu.get_barrier_semaphore()
    for peer in greet:
        pl.semaphore_signal(barrier, inc=1, device_id=peer, device_id_type=MESH)

    for load in loads[:5]:
        load.wait()
    wide = lax.broadcasted_iota(jnp.int32, (512, HID), 0) // 16
    wide = wide % 16 * 2 + wide // 16
    sel_l = (wide == lax.broadcasted_iota(jnp.int32, (512, HID), 1)).astype(F32)
    wide = lax.broadcasted_iota(jnp.int32, (128, HID), 0) % 32
    sel_r = (wide == lax.broadcasted_iota(jnp.int32, (128, HID), 1)).astype(F32)
    w_l = jnp.dot(sel_l.astype(BF), w1_ref[...], preferred_element_type=F32).astype(BF)
    w_r = jnp.dot(sel_r.astype(BF), w2_ref[...], preferred_element_type=F32).astype(BF)
    across = (((1,), (1,)), ((), ()))
    exact = dict(precision=lax.Precision.HIGHEST, preferred_element_type=F32)
    b_l = lax.dot_general(b1_ref[...], sel_l, across, **exact)
    b_r = lax.dot_general(b2_ref[...], sel_r, across, **exact)
    scale = scale_ref[...]

    loads[5].wait()

    def norm(i):
        rows = pl.ds(i * CHUNK, CHUNK)
        x = x_v[rows, :].astype(F32)
        mean = jnp.sum(x, axis=1, keepdims=True) * (1.0 / FEAT)
        dev = x - mean
        var = jnp.sum(dev * dev, axis=1, keepdims=True) * (1.0 / FEAT)
        normed = (dev * lax.rsqrt(var + 1e-5) * scale).astype(BF)
        p_l = lax.dot_general(normed, w_l, across, preferred_element_type=F32)
        for c4 in range(LC):
            proj[c4, rows, :] = p_l[:, c4 * 128 : c4 * 128 + 128]
        proj[LC, rows, :] = lax.dot_general(
            normed, w_r, across, preferred_element_type=F32
        )

    for i in range(SEQ * RES // CHUNK):
        norm(i)

    lane = lax.broadcasted_iota(jnp.int32, (RES // 4, 128), 1) // 32
    for s in range(SEQ):
        got = proj[LC, pl.ds(s * RES, RES // 4, stride=4), :]
        for p in range(1, 4):
            piece = proj[LC, pl.ds(s * RES + p, RES // 4, stride=4), :]
            got = jnp.where(lane == p, piece, got)
        got = got + b_r
        for c in range(NCOL):
            pay_f[pl.ds(c * RPAY + s * RG, RG), :] = got[c * RG : c * RG + RG]
    rpay[...] = pay_f[: NCOL * RPAY, :].astype(BF).reshape(NCOL, RPAY, 128)
    pl.semaphore_wait(barrier, len(greet))
    s1_r = []
    for n, c in enumerate(r_peers):
        n += len(l_peers)
        s1_r.append(
            pltpu.make_async_remote_copy(
                src_ref=rpay.at[c], dst_ref=rrecv.at[col],
                send_sem=s1_send.at[n], recv_sem=s1_recv.at[n],
                device_id=(row, c), device_id_type=MESH,
            )
        )
        s1_r[-1].start()
    rrecv[col] = rpay[col]

    lane = lax.broadcasted_iota(jnp.int32, (RES // 16, 128), 1) % 16
    for s in range(SEQ):
        for c4 in range(LC):
            got = proj[c4, pl.ds(s * RES, RES // 16, stride=16), :]
            for p in range(1, 16):
                piece = proj[c4, pl.ds(s * RES + p, RES // 16, stride=16), :]
                got = jnp.where(lane == p, piece, got)
            got = got + b_l[:, c4 * 128 : c4 * 128 + 128]
            for r in range(NROW):
                pay_f[pl.ds(r * LPAY + (s * LC + c4) * LB, LB), :] = got[r * LB : r * LB + LB]
    lpay[...] = pay_f[: NROW * LPAY, :].astype(BF).reshape(NROW, LPAY, 128)
    s1_l = []
    for n, (_, r, c) in enumerate(l_peers):
        s1_l.append(
            pltpu.make_async_remote_copy(
                src_ref=lpay.at[r], dst_ref=lrecv.at[at["yl"], row],
                send_sem=s1_send.at[n], recv_sem=s1_recv.at[n],
                device_id=(r, c), device_id_type=MESH,
            )
        )
        s1_l[-1].start()
    lrecv[at["yl"], row] = lpay[row]

    loads[6].wait()
    loads[7].wait()
    bd[...] = jnp.zeros_like(bd)

    def spread(p, carry):
        for half in range(2):
            for place in range(2):
                c = 2 * p + (place ^ half)
                rows = wf_v[pl.ds(pl.multiple_of(c * HID, HID), HID), :]
                for q in range(2):
                    at_row = pl.multiple_of(p * 128 + place * 64 + q * HID, HID)
                    bd[half, pl.ds(at_row, HID), q * 128 : q * 128 + 128] = rows
        return carry

    lax.fori_loop(0, HID // 2, spread, 0, unroll=4)

    k, yl, z = at["k"], at["yl"], at["z"]
    sends_l, sends_r, sends_k = {}, {}, {}

    def copy_out(ref, sends, sems, key, step):
        n = len(sends)
        copy = pltpu.make_async_remote_copy(
            src_ref=ref, dst_ref=ref, send_sem=sems[0].at[n], recv_sem=sems[1].at[n],
            device_id=spot(at, **step), device_id_type=MESH,
        )
        copy.start()
        sends[key] = copy

    def tiles(part, away):
        lo, hi = PARTS[part]
        return left.at[pl.ds(lo, hi - lo), k, pl.ds(lax.rem(z + away, 4) * 2, 2)]

    def ring_l(part):
        for step in RING:
            copy_out(tiles(part, 0), sends_l, (l_send, l_recv), (part, step), dict(z=step))

    def other_core(part, away):
        copy_out(tiles(part, away), sends_k, (k_send, k_recv), (part, away), dict(k=1))

    def arrived_l(part):
        for step in RING:
            sends_l[part, step].wait_recv()
            other_core(part, (4 - step) % 4)

    def right_of(y):
        return right.at[lax.rem(at["yh"] + y, 2) * 4 + at["x"]]

    def ring_r(y):
        for step in RING:
            copy_out(right_of(y), sends_r, (r_send, r_recv), (y, step), dict(x=step))

    for copy in s1_r:
        copy.wait_recv()
    pay_f[: NCOL * RPAY, :] = rrecv[...].reshape(NCOL * RPAY, 128).astype(F32)
    for g in range(RG):
        parts = [pay_f[pl.ds(s * RG + g, NCOL, stride=RPAY), :] for s in range(SEQ)]
        right[row, g] = jnp.concatenate(parts, axis=0).astype(BF)
    copy_out(right_of(0), sends_r, (r_send, r_recv), "y", dict(yh=1))
    ring_r(0)

    for copy in s1_l:
        copy.wait_recv()
    for y in range(2):
        pay_f[: NROW * LPAY, :] = lrecv[y].reshape(NROW * LPAY, 128).astype(F32)
        for b in range(LB):
            for c4 in range(LC):
                parts = [
                    pay_f[pl.ds((s * LC + c4) * LB + b, NROW, stride=LPAY), :] for s in range(SEQ)
                ]
                left[b, k, z * 2 + y, c4] = jnp.concatenate(parts, axis=0).astype(BF)
    ring_l(0)
    other_core(0, 0)
    other_core(1, 0)

    sends_r["y"].wait_recv()
    ring_r(1)
    ring_l(1)
    arrived_l(0)
    for y in range(2):
        for step in RING:
            sends_r[y, step].wait_recv()

    new = lax.broadcasted_iota(jnp.int32, (TOTAL, TOTAL), 0)
    old = lax.broadcasted_iota(jnp.int32, (TOTAL, TOTAL), 1)
    from_col = new // 16 % 2 * 8 + new // 32 % 4 * 2 + new // 128
    perm = (new % 8 * 32 + new // 8 % 2 * 16 + from_col == old).astype(F32).astype(BF)
    for g in range(RG):
        block = jnp.dot(
            perm, right[:, g].reshape(TOTAL, 128), preferred_element_type=F32
        ).astype(BF)
        at_lane = g * 128
        rp[0, :, at_lane : at_lane + 128] = block
        rp[1, :, at_lane : at_lane + 64] = block[:, 64:]
        rp[1, :, at_lane + 64 : at_lane + 128] = block[:, :64]

    low = lax.broadcasted_iota(jnp.int32, (256, 256), 1) % 128 < 64

    def outer(b):
        for c4 in range(LC):
            lt[b * 512 + c4 * 128 : b * 512 + c4 * 128 + 128, :] = jnp.transpose(
                left[b, :, :, c4].reshape(TOTAL, 128)
            )
        for n in range(RG // 2):
            even, odd = (
                jnp.dot(
                    lt[b * 512 + h * 256 : b * 512 + h * 256 + 256, :],
                    rp[h, :, n * 256 : n * 256 + 256],
                    preferred_element_type=F32,
                ).astype(BF)
                for h in range(2)
            )
            for half, x in enumerate((jnp.where(low, even, odd), jnp.where(low, odd, even))):
                for p in range(HID // 2):
                    for g in range(2):
                        at_row = (b * RG + 2 * n + g) * 16
                        xk[half, at_row : at_row + 16, p * 128 : p * 128 + 128] = x[
                            p * 16 : p * 16 + 16, g * 128 : g * 128 + 128
                        ]

    def project(part):
        lo, hi = PARTS[part]
        for half in range(2):
            r = jnp.dot(
                xk[half, lo * 16 * RG : hi * 16 * RG, :], bd[half], preferred_element_type=F32
            ) * (1.0 / TOTAL)
            for b in range(hi - lo):
                for g in range(RG):
                    for q in range(2):
                        at_row = (lo + b) * 16 * COLS + g * 4 + half * 2 + q
                        from_row = (b * RG + g) * 16
                        out_ref[pl.ds(at_row, 16, stride=COLS), :] = r[
                            from_row : from_row + 16, q * 128 : q * 128 + 128
                        ] + bf_ref[...]

    def from_core(part):
        for away in range(4):
            sends_k[part, away].wait_recv()

    from_core(0)
    for b in range(*PARTS[0]):
        outer(b)
    arrived_l(1)
    project(0)
    from_core(1)
    for b in range(*PARTS[1]):
        outer(b)
    project(1)

    for sends in (sends_l, sends_r, sends_k):
        for copy in sends.values():
            copy.wait_send()
    for copy in s1_l + s1_r:
        copy.wait_send()


def body(x, scale, w1, b1, w2, b2, wf, bf, pair):
    vmem = pl.BlockSpec(memory_space=pltpu.VMEM)
    hbm = pl.BlockSpec(memory_space=pltpu.HBM)
    dma = pltpu.SemaphoreType.DMA
    n1 = 2 * NROW - 1 + NCOL - 1
    acc = pl.pallas_call(
        kernel,
        out_shape=pltpu.VMEM((ROWS * COLS, CP), F32),
        in_specs=[hbm] * 8,
        out_specs=vmem,
        scratch_shapes=[
            pltpu.VMEM((SEQ * RES, FEAT), BF),
            pltpu.VMEM((1, FEAT), F32),
            pltpu.VMEM((HID, FEAT), BF),
            pltpu.VMEM((1, HID), F32),
            pltpu.VMEM((HID, FEAT), BF),
            pltpu.VMEM((1, HID), F32),
            pltpu.VMEM((HID * HID, CP), BF),
            pltpu.VMEM((1, CP), F32),
            pltpu.VMEM((5, SEQ * RES, 128), F32),
            pltpu.VMEM((NCOL * RPAY, 128), F32),
            pltpu.VMEM((NROW, LPAY, 128), BF),
            pltpu.VMEM((NCOL, RPAY, 128), BF),
            pltpu.VMEM((2, NROW, LPAY, 128), BF),
            pltpu.VMEM((NCOL, RPAY, 128), BF),
            pltpu.VMEM((LB, 2, 8, LC, SEQ * NROW, 128), BF),
            pltpu.VMEM((NROW, RG, SEQ * NCOL, 128), BF),
            pltpu.VMEM((ROWS * HID, TOTAL), BF),
            pltpu.VMEM((2, TOTAL, COLS * HID), BF),
            pltpu.VMEM((2, RG * ROWS, HID * 64), BF),
            pltpu.VMEM((2, HID * 64, 2 * CP), BF),
            dma((8,)), dma((n1,)), dma((n1,)),
            dma((6,)), dma((6,)), dma((7,)), dma((7,)), dma((8,)), dma((8,)),
        ],
        compiler_params=pltpu.CompilerParams(
            collective_id=0, has_side_effects=True, vmem_limit_bytes=56 * 2**20
        ),
    )(
        x.reshape(SEQ * RES, FEAT), scale.reshape(1, FEAT), w1.T, b1.reshape(1, HID),
        w2.T, b2.reshape(1, HID), wf, bf.reshape(1, CP),
    )
    return (pair.astype(F32) + acc.reshape(ROWS, COLS, CP)).astype(BF)


def solution(mesh):
    return jax.shard_map(
        body,
        mesh=mesh,
        in_specs=(P(("row", "col"), None, None), P(), P(), P(), P(), P(), P(), P(), P("row", "col", None)),
        out_specs=P("row", "col", None),
        check_vma=False,
    )
```

time: 33.5 us -> 30.4 us (0.907)
  Pallas kernels: 32.3 us -> 29.2 us
    pallas_call x1, Pallas kernels: 32.3 us -> 29.2 us  [body(): pl.pallas_call(kernel, out_shape=pltpu.VMEM((ROWS * COLS, CP), F32), in_s...]
where the time goes in v2:
time: 30.4 us; the launch traced here: 30.3 us
  Pallas kernels  29.2 us (96%)
  other arithmetic  1.05 us (3%)
    pallas_call x1, Pallas kernels, body(): pl.pallas_call(kernel, out_shape=pltpu.VMEM((ROWS * COLS, CP), F32), in_s...  29.2 us
    convert_element_type x1, other arithmetic, body(): return (pair.astype(F32) + acc.reshape(ROWS, COLS, CP)).astype(BF)  1.05 us

profile of v2, /device:TPU:1, one launch (start us, length us, event | category | flops | bytes accessed | tf_op | source)
XLA Modules:
  0.0 30.3 jit_solution(4687172602409407614)
XLA Ops:
  0.0 0.0 copy-start
  0.0 29.2 %shard_map.91 = f32[3200,128]{1,0:T(8,128)S(1)} custom-call(bf16[1280,256]{1,0:T(8,128)(2,1)} %bitcast.9, f32[1,256]{1,0:T(1,128)} %bitcast.12, bf16[32,256]{1,0:T(8,128)(2,1)} %bitcast.10, f32[1,32]{1,0:T(1,128)} %bitcast.13, bf16[32,256]{1,0:T(8,128)(2,1)} %bitcast.11, f32[1,32]{1,0:T(1,128)} %bitcast.14, bf16[1024,128]{1,0:T(8,128)(2,1)} %wf_hbm.1, ...), custom_call_target="tpu_custom_call" | custom-call | tf_op jit(solution)/shard_map/pallas_call | solution.py:304
  29.2 0.0 copy-done
  29.2 1.1 %add_convert_fusion = bf16[80,40,128]{2,1,0:T(8,128)(2,1)} fusion(f32[80,40,128]{2,1,0:T(8,128)S(1)} %bitcast.8, bf16[80,40,128]{2,1,0:T(8,128)(2,1)S(1)} %copy-done), kind=kLoop, calls=%fused_computation | loop fusion | flops 1228800 | bytes 3276800 | tf_op jit(solution)/shard_map/convert_element_type | solution.py:340
Async XLA Ops:
  0.0 29.2 %copy-start = (bf16[80,40,128]{2,1,0:T(8,128)(2,1)S(1)}, bf16[80,40,128]{2,1,0:T(8,128)(2,1)}, u32[]{:S(2)}) copy-start(bf16[80,40,128]{2,1,0:T(8,128)(2,1)} %param.17) | copy-start | bytes 2457604

commit v3 on v2

--- a/solution.py
+++ b/solution.py
@@ -21,8 +21,7 @@
 LB, LC = ROWS // 16, HID // 8
 LT = LB * LC
 RG = COLS // 4
-RING = (2, 1, 3)
-PARTS = ((0, 3), (3, 5))
+PARTS = ((0, 2), (2, 4), (4, 5))
 LPAY, RPAY = 48, 32
 CHUNK = 320
 
@@ -34,8 +33,8 @@
 
 
 def kernel(
-    x_hbm, scale_hbm, w1_hbm, b1_hbm, w2_hbm, b2_hbm, wf_hbm, bf_hbm, out_ref,
-    x_v, scale_ref, w1_ref, b1_ref, w2_ref, b2_ref, wf_v, bf_ref, proj, pay_f, lpay, rpay, lrecv, rrecv, left, right,
+    x_hbm, scale_hbm, w1_hbm, b1_hbm, w2_hbm, b2_hbm, wf_hbm, bf_hbm, pair_hbm, out_ref,
+    x_v, scale_ref, w1_ref, b1_ref, w2_ref, b2_ref, wf_v, bf_ref, pair_v, acc, proj, pay_f, lpay, rpay, lrecv, rrecv, left, right,
     lt, rp, xk, bd,
     load_sem, s1_send, s1_recv, l_send, l_recv, r_send, r_recv, k_send, k_recv,
 ):
@@ -47,6 +46,7 @@
         for n, (source, held) in enumerate((
             (w1_hbm, w1_ref), (w2_hbm, w2_ref), (b1_hbm, b1_ref), (b2_hbm, b2_ref),
             (scale_hbm, scale_ref), (x_hbm, x_v), (wf_hbm, wf_v), (bf_hbm, bf_ref),
+            (pair_hbm, pair_v),
         ))
     ]
     for load in loads:
@@ -141,8 +141,8 @@
         s1_l[-1].start()
     lrecv[at["yl"], row] = lpay[row]
 
-    loads[6].wait()
-    loads[7].wait()
+    for load in loads[6:]:
+        load.wait()
     bd[...] = jnp.zeros_like(bd)
 
     def spread(p, carry):
@@ -173,24 +173,35 @@
         lo, hi = PARTS[part]
         return left.at[pl.ds(lo, hi - lo), k, pl.ds(lax.rem(z + away, 4) * 2, 2)]
 
+    def out_l(key, ref, **step):
+        copy_out(ref, sends_l, (l_send, l_recv), key, step)
+
+    def out_r(key, ref, **step):
+        copy_out(ref, sends_r, (r_send, r_recv), key, step)
+
+    def out_k(key, ref):
+        copy_out(ref, sends_k, (k_send, k_recv), key, dict(k=1))
+
     def ring_l(part):
-        for step in RING:
-            copy_out(tiles(part, 0), sends_l, (l_send, l_recv), (part, step), dict(z=step))
-
-    def other_core(part, away):
-        copy_out(tiles(part, away), sends_k, (k_send, k_recv), (part, away), dict(k=1))
+        for step in (2, 1, 3):
+            out_l((part, step), tiles(part, 0), z=step)
+        out_k((part, 0), tiles(part, 0))
+
+    def sent_l(part):
+        for step in (2, 1, 3):
+            sends_l.get((part, step)).wait_send()
 
     def arrived_l(part):
-        for step in RING:
+        for step in (2, 1, 3):
             sends_l[part, step].wait_recv()
-            other_core(part, (4 - step) % 4)
-
-    def right_of(y):
-        return right.at[lax.rem(at["yh"] + y, 2) * 4 + at["x"]]
-
-    def ring_r(y):
-        for step in RING:
-            copy_out(right_of(y), sends_r, (r_send, r_recv), (y, step), dict(x=step))
+            out_k((part, step), tiles(part, 4 - step))
+
+    def right_of(y, x):
+        return right.at[lax.rem(at["yh"] + y, 2) * 4 + lax.rem(at["x"] + x, 4)]
+
+    def near_r(y):
+        for step in (1, 3):
+            out_r((y, step), right_of(y, 0), x=step)
 
     for copy in s1_r:
         copy.wait_recv()
@@ -198,8 +209,9 @@
     for g in range(RG):
         parts = [pay_f[pl.ds(s * RG + g, NCOL, stride=RPAY), :] for s in range(SEQ)]
         right[row, g] = jnp.concatenate(parts, axis=0).astype(BF)
-    copy_out(right_of(0), sends_r, (r_send, r_recv), "y", dict(yh=1))
-    ring_r(0)
+    out_r("y", right_of(0, 0), yh=1)
+    out_r((0, 2), right_of(0, 0), x=2)
+    near_r(0)
 
     for copy in s1_l:
         copy.wait_recv()
@@ -212,16 +224,24 @@
                 ]
                 left[b, k, z * 2 + y, c4] = jnp.concatenate(parts, axis=0).astype(BF)
     ring_l(0)
-    other_core(0, 0)
-    other_core(1, 0)
 
     sends_r["y"].wait_recv()
-    ring_r(1)
+    near_r(1)
+    sent_l(0)
     ring_l(1)
+    sends_r[0, 2].wait_recv()
+    out_r((1, 2), right_of(0, 2), yh=1)
     arrived_l(0)
-    for y in range(2):
-        for step in RING:
-            sends_r[y, step].wait_recv()
+    sent_l(1)
+    ring_l(2)
+    for key in ((0, 1), (0, 3), (1, 1), (1, 3), (1, 2)):
+        sends_r[key].wait_recv()
+
+    def from_core(part):
+        for key in range(4):
+            sends_k[part, key].wait_recv()
+
+    from_core(0)
 
     new = lax.broadcasted_iota(jnp.int32, (TOTAL, TOTAL), 0)
     old = lax.broadcasted_iota(jnp.int32, (TOTAL, TOTAL), 1)
@@ -265,31 +285,35 @@
         for half in range(2):
             r = jnp.dot(
                 xk[half, lo * 16 * RG : hi * 16 * RG, :], bd[half], preferred_element_type=F32
-            ) * (1.0 / TOTAL)
+            )
             for b in range(hi - lo):
                 for g in range(RG):
                     for q in range(2):
                         at_row = (lo + b) * 16 * COLS + g * 4 + half * 2 + q
                         from_row = (b * RG + g) * 16
-                        out_ref[pl.ds(at_row, 16, stride=COLS), :] = r[
+                        acc[pl.ds(at_row, 16, stride=COLS), :] = r[
                             from_row : from_row + 16, q * 128 : q * 128 + 128
-                        ] + bf_ref[...]
-
-    def from_core(part):
-        for away in range(4):
-            sends_k[part, away].wait_recv()
-
-    from_core(0)
-    for b in range(*PARTS[0]):
-        outer(b)
+                        ]
+        rows = slice(lo * 16 * COLS, hi * 16 * COLS)
+        update = acc[rows, :] * (1.0 / TOTAL) + bf_ref[...]
+        out_ref[rows, :] = (pair_v[rows, :].astype(F32) + update).astype(BF)
+
+    outer(0)
     arrived_l(1)
+    outer(1)
+    arrived_l(2)
     project(0)
     from_core(1)
     for b in range(*PARTS[1]):
         outer(b)
     project(1)
-
-    for sends in (sends_l, sends_r, sends_k):
+    from_core(2)
+    for b in range(*PARTS[2]):
+        outer(b)
+    project(2)
+
+    sent_l(2)
+    for sends in (sends_r, sends_k):
         for copy in sends.values():
             copy.wait_send()
     for copy in s1_l + s1_r:
@@ -301,10 +325,10 @@
     hbm = pl.BlockSpec(memory_space=pltpu.HBM)
     dma = pltpu.SemaphoreType.DMA
     n1 = 2 * NROW - 1 + NCOL - 1
-    acc = pl.pallas_call(
+    out = pl.pallas_call(
         kernel,
-        out_shape=pltpu.VMEM((ROWS * COLS, CP), F32),
-        in_specs=[hbm] * 8,
+        out_shape=pltpu.VMEM((ROWS * COLS, CP), BF),
+        in_specs=[hbm] * 9,
         out_specs=vmem,
         scratch_shapes=[
             pltpu.VMEM((SEQ * RES, FEAT), BF),
@@ -315,6 +339,8 @@
             pltpu.VMEM((1, HID), F32),
             pltpu.VMEM((HID * HID, CP), BF),
             pltpu.VMEM((1, CP), F32),
+            pltpu.VMEM((ROWS * COLS, CP), BF),
+            pltpu.VMEM((ROWS * COLS, CP), F32),
             pltpu.VMEM((5, SEQ * RES, 128), F32),
             pltpu.VMEM((NCOL * RPAY, 128), F32),
             pltpu.VMEM((NROW, LPAY, 128), BF),
@@ -327,8 +353,8 @@
             pltpu.VMEM((2, TOTAL, COLS * HID), BF),
             pltpu.VMEM((2, RG * ROWS, HID * 64), BF),
             pltpu.VMEM((2, HID * 64, 2 * CP), BF),
-            dma((8,)), dma((n1,)), dma((n1,)),
-            dma((6,)), dma((6,)), dma((7,)), dma((7,)), dma((8,)), dma((8,)),
+            dma((9,)), dma((n1,)), dma((n1,)),
+            dma((9,)), dma((9,)), dma((7,)), dma((7,)), dma((12,)), dma((12,)),
         ],
         compiler_params=pltpu.CompilerParams(
             collective_id=0, has_side_effects=True, vmem_limit_bytes=56 * 2**20
@@ -336,8 +362,9 @@
     )(
         x.reshape(SEQ * RES, FEAT), scale.reshape(1, FEAT), w1.T, b1.reshape(1, HID),
         w2.T, b2.reshape(1, HID), wf, bf.reshape(1, CP),
+        pair.reshape(ROWS * COLS, CP),
     )
-    return (pair.astype(F32) + acc.reshape(ROWS, COLS, CP)).astype(BF)
+    return out.reshape(ROWS, COLS, CP)
 
 
 def solution(mesh):

time: 30.4 us -> 29.8 us (0.980)
  other arithmetic: 1.05 us -> 0 us
  local copies, waits for them, and re-layouts: 0.01 us -> 0.89 us
  Pallas kernels: 29.2 us -> 28.7 us
    convert_element_type x1 -> x0, other arithmetic: 1.05 us -> none  [body(): return (pair.astype(F32) + acc.reshape(ROWS, COLS, CP)).astype(BF)]
    unnamed x2 -> x1, local copies, waits for them, and re-layouts: 0.01 us -> 0.89 us
    pallas_call x1, Pallas kernels: 29.2 us -> 28.7 us  [body(): pl.pallas_call(kernel, out_shape=pltpu.VMEM((ROWS * COLS, CP), BF), in_sp...]
where the time goes in v3:
time: 29.8 us; the launch traced here: 29.6 us
  Pallas kernels  28.7 us (96%)
  local copies, waits for them, and re-layouts  0.89 us (3%)
    pallas_call x1, Pallas kernels, body(): pl.pallas_call(kernel, out_shape=pltpu.VMEM((ROWS * COLS, CP), BF), in_sp...  28.7 us
    unnamed x1, local copies, waits for them, and re-layouts  0.89 us

profile of v3, /device:TPU:1, one launch (start us, length us, event | category | flops | bytes accessed | tf_op | source)
XLA Modules:
  0.0 29.6 jit_solution(15901961697928378416)
XLA Ops:
  0.0 28.7 %shard_map.91 = bf16[3200,128]{1,0:T(8,128)(2,1)S(1)} custom-call(bf16[1280,256]{1,0:T(8,128)(2,1)} %bitcast.11, f32[1,256]{1,0:T(1,128)} %bitcast.14, bf16[32,256]{1,0:T(8,128)(2,1)} %bitcast.12, f32[1,32]{1,0:T(1,128)} %bitcast.15, bf16[32,256]{1,0:T(8,128)(2,1)} %bitcast.13, f32[1,32]{1,0:T(1,128)} %bitcast.16, bf16[1024,128]{1,0:T(8,128)(2,1)} %wf_hbm.1, ...), custom_call_target="tpu_custom_call" | custom-call | tf_op jit(solution)/shard_map/pallas_call | solution.py:328
  28.7 0.9 %copy.11 = bf16[80,40,128]{2,1,0:T(8,128)(2,1)} copy(bf16[80,40,128]{2,1,0:T(8,128)(2,1)S(1)} %bitcast.9) | data formatting | bytes 1638400

commit v4 on v3

--- a/solution.py
+++ b/solution.py
@@ -301,8 +301,8 @@
     outer(0)
     arrived_l(1)
     outer(1)
+    project(0)
     arrived_l(2)
-    project(0)
     from_core(1)
     for b in range(*PARTS[1]):
         outer(b)

time: 29.8 us -> 29.7 us (level)
  no operation moved by 1% of the time
where the time goes in v4:
time: 29.7 us; the launch traced here: 29.6 us
  Pallas kernels  28.7 us (97%)
  local copies, waits for them, and re-layouts  0.89 us (3%)
    pallas_call x1, Pallas kernels, body(): pl.pallas_call(kernel, out_shape=pltpu.VMEM((ROWS * COLS, CP), BF), in_sp...  28.7 us
    unnamed x1, local copies, waits for them, and re-layouts  0.89 us

profile of v4, /device:TPU:1, one launch (start us, length us, event | category | flops | bytes accessed | tf_op | source)
XLA Modules:
  0.0 29.6 jit_solution(17989537983886734351)
XLA Ops:
  0.0 28.7 %shard_map.91 = bf16[3200,128]{1,0:T(8,128)(2,1)S(1)} custom-call(bf16[1280,256]{1,0:T(8,128)(2,1)} %bitcast.11, f32[1,256]{1,0:T(1,128)} %bitcast.14, bf16[32,256]{1,0:T(8,128)(2,1)} %bitcast.12, f32[1,32]{1,0:T(1,128)} %bitcast.15, bf16[32,256]{1,0:T(8,128)(2,1)} %bitcast.13, f32[1,32]{1,0:T(1,128)} %bitcast.16, bf16[1024,128]{1,0:T(8,128)(2,1)} %wf_hbm.1, ...), custom_call_target="tpu_custom_call" | custom-call | tf_op jit(solution)/shard_map/pallas_call | solution.py:328
  28.7 0.9 %copy.11 = bf16[80,40,128]{2,1,0:T(8,128)(2,1)} copy(bf16[80,40,128]{2,1,0:T(8,128)(2,1)S(1)} %bitcast.9) | data formatting | bytes 1638400
